TPU v7x, 32 devices: a whole 2x2x4 slice. The times are simulated.
32 devices in a mesh: grp: 2 (over y), tm: 4 (over z), sub: 2 (over x), ch: 2 (over core).
Axes of the slice: x: 2, y: 2, z: 4, core: 2. Of those that a mesh axis runs over, the one named last changes fastest.
Arguments:
- archive: float32 [16, 16384], P('ch', ('grp', 'tm')), parts along dimension 1, may hold values from -6 to 6
- tail: float32 [16, 254], P(None, 'grp'), parts along dimension 1, may hold values from -6 to 6
- precision: float32 [16, 16], replicated, may hold values from -1.5 to 1.5
- tile_list: int32 [8, 2, 2, 2], P(('grp', 'tm'), 'sub'), parts along dimension 0, may hold values from 0 to 15, as said below
Outputs:
- profile: float32 [16384], P(('grp', 'tm', 'sub')), parts along dimension 0
There are 2 independent parts, one for each index of `grp`. A program takes and returns all parts, laid end to end along the dimension named above; an argument that names none is the same for every part. Nothing has to cross between parts.
Inputs may be any that keep to these rules, and one draw needn't show every extreme that they name: `tile_list`: each pair has row block <= column block; every block k < 16 appears in some pair; pairs may repeat.
All inputs are finite; a program needn't handle non-finite values.
Results may differ from a plain program's by a relative error of at most 0.0003.
Values may be sent and summed in bfloat16 or wider, within the bound.
A program may use at most 128 MiB of HBM per device.

v0:
```python
import functools

import jax
import jax.numpy as jnp
from jax import lax
from jax.experimental import pallas as pl
from jax.experimental.pallas import tpu as pltpu
from jax.sharding import PartitionSpec as P

M = 128
TS = 512
SLOTS = 2
DEPTH = 2048
EXCL = 32
LANES = 128
STEP = 16
COLS = TS + M
ROWS = TS // 2 + M
SPAN = COLS + ROWS
MESH = pl.DeviceIdType.MESH


def whiten(factor, samples):
    return jnp.dot(
        factor, samples, precision=lax.Precision.HIGHEST, preferred_element_type=jnp.float32
    ).astype(jnp.bfloat16)


def kernel(
    n_tm,
    n_sub,
    tiles_hbm,
    archive_ref,
    tail_hbm,
    precision_hbm,
    out_ref,
    tiles_ref,
    tail_ref,
    precision_ref,
    raw_ref,
    series_ref,
    hankel_ref,
    lagged_ref,
    mine_ref,
    theirs_ref,
    load_sems,
    raw_sems,
    time_send,
    time_recv,
    pair_send,
    pair_recv,
    min_sems,
):
    tm, sub, ch = lax.axis_index("tm"), lax.axis_index("sub"), lax.axis_index("ch")
    other = 1 - ch
    group = n_tm * n_sub * 2
    me = (tm * n_sub + sub) * 2 + ch
    channels, span = archive_ref.shape
    half = span // 2
    starts_all = n_tm * span

    def place(rank):
        owner = rank // 2
        return {"tm": owner // n_sub, "sub": owner % n_sub, "ch": rank % 2}

    def each_peer(action):
        if group <= 16:
            for step in range(1, group):
                action(step)
        else:
            lax.fori_loop(1, group, lambda step, _: (action(step), 0)[1], 0)

    own_rows = pl.ds(pl.multiple_of(ch * channels, channels), channels)
    own_half = archive_ref.at[:, pl.ds(pl.multiple_of(ch * half, half), half)]
    loads = [
        pltpu.make_async_copy(source, target, load_sems.at[at])
        for at, (source, target) in enumerate(
            (
                (precision_hbm, precision_ref),
                (tail_hbm, tail_ref),
                (own_half, raw_ref.at[own_rows, :]),
                (tiles_hbm, tiles_ref),
            )
        )
    ]
    for load in loads:
        load.start()
    barrier = pltpu.get_barrier_semaphore()
    each_peer(
        lambda step: pl.semaphore_signal(
            barrier, inc=1, device_id=place(lax.rem(me + step, group)), device_id_type=MESH
        )
    )
    for load in loads[:2]:
        load.wait()
    factor = precision_ref[...]
    last = starts_all // LANES
    series_ref[last] = jnp.zeros((2 * channels, LANES), jnp.bfloat16)
    series_ref[last, :, : M - 1] = whiten(factor, tail_ref[...])
    pl.semaphore_wait(barrier, group - 1)

    swap = pltpu.make_async_remote_copy(
        src_ref=archive_ref.at[:, pl.ds(pl.multiple_of(other * half, half), half)],
        dst_ref=raw_ref.at[own_rows, :],
        send_sem=raw_sems.at[0],
        recv_sem=raw_sems.at[1],
        device_id={"ch": other},
        device_id_type=MESH,
    )
    swap.start()
    for load in loads[2:]:
        load.wait()
    swap.wait_recv()

    tiles = half // LANES

    def chunk(owner, part):
        return series_ref.at[pl.ds((owner * 2 + part) * tiles, tiles)]

    mine = chunk(tm, ch)
    whitened = whiten(factor, raw_ref[...])
    for k in range(tiles):
        series_ref[(tm * 2 + ch) * tiles + k] = whitened[:, k * LANES : (k + 1) * LANES]
    along_time = [None]
    for back in range(1, n_tm):
        along_time.append(
            pltpu.make_async_remote_copy(
                src_ref=mine,
                dst_ref=mine,
                send_sem=time_send.at[back],
                recv_sem=time_recv.at[back],
                device_id={"tm": lax.rem(tm + back, n_tm)},
                device_id_type=MESH,
            )
        )
        along_time[back].start()
    to_pair = []
    for back in range(n_tm):
        if back:
            along_time[back].wait_recv()
        held = chunk(lax.rem(tm + n_tm - back, n_tm), ch)
        to_pair.append(
            pltpu.make_async_remote_copy(
                src_ref=held,
                dst_ref=held,
                send_sem=pair_send.at[back],
                recv_sem=pair_recv.at[back],
                device_id={"ch": other},
                device_id_type=MESH,
            )
        )
        to_pair[back].start()
    for copy in to_pair:
        copy.wait_recv()

    pieces = []
    for slot in range(SLOTS):
        per_block = TS // LANES
        row_tile = tiles_ref[0, 0, slot, 0] * per_block + ch * (per_block // 2)
        col_tile = tiles_ref[0, 0, slot, 1] * per_block
        pieces.extend(series_ref[col_tile + k] for k in range(COLS // LANES))
        pieces.extend(series_ref[row_tile + k] for k in range(ROWS // LANES))
    segment = jnp.concatenate(pieces, axis=1).astype(jnp.float32)
    width = segment.shape[1]
    depth = segment.shape[0]
    for lag in range(STEP):
        moved = segment if lag == 0 else pltpu.roll(segment, width - lag, axis=1)
        hankel_ref[lag * depth : (lag + 1) * depth, :] = moved.astype(jnp.bfloat16)
    size = STEP * depth
    unit = (
        lax.broadcasted_iota(jnp.int32, (size, size), 0)
        == lax.broadcasted_iota(jnp.int32, (size, size), 1)
    ).astype(jnp.bfloat16)
    for at in range(0, width, size):
        lagged_ref[at : at + size, :] = lax.dot_general(
            unit,
            hankel_ref[:, at : at + size],
            (((1,), (1,)), ((), ())),
            preferred_element_type=jnp.float32,
        ).astype(jnp.bfloat16)
    norms = jnp.broadcast_to(jnp.sum(segment * segment, axis=0, keepdims=True), (8, width))
    shift = 1
    while shift < M:
        norms = norms + pltpu.roll(norms, width - shift, axis=1)
        shift *= 2

    owners, piece_rows, _ = mine_ref.shape
    place_shape = (owners, piece_rows, LANES)
    line = lax.broadcasted_iota(jnp.int32, place_shape, 0) * piece_rows
    line = line + lax.broadcasted_iota(jnp.int32, place_shape, 1)
    block_of, part_of = line // per_block, line % per_block
    best = jnp.full(place_shape, jnp.inf, jnp.float32)
    for slot in range(SLOTS):
        col_at = slot * SPAN
        row_at = col_at + COLS
        n_rows = TS // 2
        left = jnp.concatenate(
            [lagged_ref[row_at + v : row_at + v + n_rows, :] for v in range(0, M, STEP)], axis=1
        )
        right = jnp.concatenate(
            [lagged_ref[col_at + v : col_at + v + TS, :] for v in range(0, M, STEP)], axis=1
        )
        products = lax.dot_general(
            left, right, (((1,), (1,)), ((), ())), preferred_element_type=jnp.float32
        )
        row_block = tiles_ref[0, 0, slot, 0]
        col_block = tiles_ref[0, 0, slot, 1]
        between = row_block * TS + ch * n_rows - col_block * TS
        separation = (
            lax.broadcasted_iota(jnp.int32, (n_rows, TS), 0)
            - lax.broadcasted_iota(jnp.int32, (n_rows, TS), 1)
            + between
        )
        scores = jnp.where(jnp.abs(separation) < EXCL, jnp.inf, -2.0 * products)
        row_norms = norms[:1, row_at : row_at + n_rows]
        col_norms = norms[:1, col_at : col_at + TS]
        row_wide = jnp.transpose(jnp.broadcast_to(row_norms, (LANES, n_rows)))
        by_col = jnp.min(scores + jnp.concatenate([row_wide] * per_block, axis=1), axis=0, keepdims=True)
        by_col = (by_col + col_norms) * (1.0 / DEPTH)
        with_col = scores + col_norms
        folded = with_col[:, :LANES]
        for q in range(1, per_block):
            folded = jnp.minimum(folded, with_col[:, q * LANES : (q + 1) * LANES])
        by_row = jnp.min(jnp.transpose(folded), axis=0, keepdims=True)
        by_row = (by_row + row_norms) * (1.0 / DEPTH)
        for q in range(per_block):
            here = by_col[:, q * LANES : (q + 1) * LANES].reshape(1, 1, LANES)
            hit = (block_of == col_block) & (part_of == q)
            best = jnp.minimum(best, jnp.where(hit, here, jnp.inf))
        for q in range(per_block // 2):
            here = by_row[:, q * LANES : (q + 1) * LANES].reshape(1, 1, LANES)
            hit = (block_of == row_block) & (part_of == q + ch * (per_block // 2))
            best = jnp.minimum(best, jnp.where(hit, here, jnp.inf))
    mine_ref[...] = best

    def send_minima(step):
        rank = lax.rem(me + step, group)
        pltpu.make_async_remote_copy(
            src_ref=mine_ref.at[rank // 2],
            dst_ref=theirs_ref.at[step - 1],
            send_sem=min_sems.at[0],
            recv_sem=min_sems.at[1],
            device_id=place(rank),
            device_id_type=MESH,
        ).start()

    each_peer(send_minima)
    every = pltpu.make_async_remote_copy(
        src_ref=theirs_ref,
        dst_ref=theirs_ref,
        send_sem=min_sems.at[0],
        recv_sem=min_sems.at[1],
        device_id={"ch": other},
        device_id_type=MESH,
    )
    every.wait_recv()
    out_ref[...] = jnp.minimum(mine_ref[me // 2], jnp.min(theirs_ref[...], axis=0))
    every.wait_send()
    swap.wait_send()
    for copy in along_time[1:] + to_pair:
        copy.wait_send()


def body(archive, tail, precision, tile_list):
    n_tm, n_sub = lax.axis_size("tm"), lax.axis_size("sub")
    group = n_tm * n_sub * 2
    channels, span = archive.shape
    starts_all = span * n_tm
    piece_rows = starts_all // (n_tm * n_sub) // LANES
    every = 2 * channels
    width = SLOTS * SPAN
    anywhere = pl.BlockSpec(memory_space=pl.ANY)
    out = pl.pallas_call(
        functools.partial(kernel, n_tm, n_sub),
        out_shape=jax.ShapeDtypeStruct((piece_rows, LANES), jnp.float32),
        in_specs=[anywhere] * 4,
        out_specs=pl.BlockSpec(memory_space=pltpu.VMEM),
        scratch_shapes=[
            pltpu.SMEM(tile_list.shape, jnp.int32),
            pltpu.VMEM(tail.shape, jnp.float32),
            pltpu.VMEM(precision.shape, jnp.float32),
            pltpu.VMEM((every, span // 2), jnp.float32),
            pltpu.VMEM((starts_all // LANES + 1, every, LANES), jnp.bfloat16),
            pltpu.VMEM((STEP * every, width), jnp.bfloat16),
            pltpu.VMEM((width, STEP * every), jnp.bfloat16),
            pltpu.VMEM((n_tm * n_sub, piece_rows, LANES), jnp.float32),
            pltpu.VMEM((group - 1, piece_rows, LANES), jnp.float32),
            pltpu.SemaphoreType.DMA((4,)),
            pltpu.SemaphoreType.DMA((2,)),
            pltpu.SemaphoreType.DMA((n_tm,)),
            pltpu.SemaphoreType.DMA((n_tm,)),
            pltpu.SemaphoreType.DMA((n_tm,)),
            pltpu.SemaphoreType.DMA((n_tm,)),
            pltpu.SemaphoreType.DMA((2,)),
        ],
        compiler_params=pltpu.CompilerParams(
            collective_id=0, has_side_effects=True, vmem_limit_bytes=60 * 2**20
        ),
    )(tile_list, archive, tail, precision)
    return out.reshape(-1)


def solution(mesh):
    placed = (P("ch", ("grp", "tm")), P(None, "grp"), P(), P(("grp", "tm"), "sub", None, None))
    return jax.shard_map(
        body, mesh=mesh, in_specs=placed, out_specs=P(("grp", "tm", "sub")), check_vma=False
    )
```

profile of v0, /device:TPU:0, one launch (start us, length us, event | category | flops | bytes accessed | tf_op | source)
XLA Modules:
  0.0 20.5 jit_solution(18330265550520952418)
XLA Ops:
  0.0 19.2 %shard_map.46 = f32[8,128]{1,0:T(8,128)} custom-call(s32[1,1,2,2]{3,2,1,0:T(2,128)} %tiles_hbm.1, f32[8,2048]{1,0:T(8,128)} %archive_ref.1, f32[16,127]{1,0:T(8,128)} %tail_hbm.1, f32[16,16]{1,0:T(8,128)} %precision_hbm.1), custom_call_target="tpu_custom_call" | custom-call | tf_op jit(solution)/shard_map/pallas_call | solution.py:273
  19.2 1.3 %copy.6 = f32[1024]{0:T(1024)} copy(f32[1024]{0:T(1024)} %bitcast.1) | data formatting | bytes 8192
where the time goes:
time: 20.7 us; the launch traced here: 20.5 us
  Pallas kernels  19.2 us (93%)
  local copies, waits for them, and re-layouts  1.28 us (6%)
    pallas_call x1, Pallas kernels, body(): pl.pallas_call(functools.partial(kernel, n_tm, n_sub), out_shape=jax.Shap...  19.2 us
    unnamed x1, local copies, waits for them, and re-layouts  1.28 us

commit v1 on v0

v1 whole, which is shorter than its diff:
```python
import functools

import jax
import jax.numpy as jnp
from jax import lax
from jax.experimental import pallas as pl
from jax.experimental.pallas import tpu as pltpu
from jax.sharding import PartitionSpec as P

M = 128
TS = 512
SLOTS = 2
DEPTH = 2048
EXCL = 32
LANES = 128
STEP = 16
MESH = pl.DeviceIdType.MESH


def whiten(factor, samples):
    return jnp.dot(
        factor, samples, precision=lax.Precision.HIGHEST, preferred_element_type=jnp.float32
    ).astype(jnp.bfloat16)


def gather_kernel(
    n_tm,
    n_sub,
    tiles_hbm,
    archive_hbm,
    tail_hbm,
    precision_hbm,
    series_ref,
    lists_ref,
    tail_ref,
    precision_ref,
    raw_ref,
    load_sems,
    raw_sems,
    time_send,
    time_recv,
    pair_send,
    pair_recv,
    list_send,
    list_recv,
    lists_send,
    lists_recv,
    time_here,
    sub_here,
):
    tm, sub, ch = lax.axis_index("tm"), lax.axis_index("sub"), lax.axis_index("ch")
    other = 1 - ch
    channels, span = archive_hbm.shape
    half = span // 2
    tiles = half // LANES
    last = n_tm * span // LANES

    def send(source, target, sem, landed, device):
        return pltpu.make_async_remote_copy(
            src_ref=source,
            dst_ref=target,
            send_sem=sem,
            recv_sem=landed,
            device_id=device,
            device_id_type=MESH,
        )

    def others(axis, size, here):
        for step in range(size - 1):
            yield step, step >= here, {axis: step + (step + size - here) // size}

    barrier = pltpu.get_barrier_semaphore()
    pl.semaphore_signal(barrier, inc=1, device_id={"ch": other}, device_id_type=MESH)
    for axis, size, here in (("tm", n_tm, tm), ("sub", n_sub, sub)):
        for step, after, device in others(axis, size, here):

            @pl.when(after)
            def _():
                pl.semaphore_signal(barrier, inc=1, device_id=device, device_id_type=MESH)

    own_rows = pl.ds(pl.multiple_of(ch * channels, channels), channels)
    own_half = archive_hbm.at[:, pl.ds(pl.multiple_of(ch * half, half), half)]
    own_list = lists_ref.at[sub, tm]
    loads = [
        pltpu.make_async_copy(source, target, load_sems.at[at])
        for at, (source, target) in enumerate(
            (
                (precision_hbm, precision_ref),
                (tail_hbm, tail_ref),
                (own_half, raw_ref.at[own_rows, :]),
                (tiles_hbm.at[0, 0], own_list),
            )
        )
    ]
    for load in loads:
        load.start()
    pl.semaphore_wait(barrier, 1 + tm + sub)

    swap = send(
        archive_hbm.at[:, pl.ds(pl.multiple_of(other * half, half), half)],
        raw_ref.at[own_rows, :],
        raw_sems.at[0],
        raw_sems.at[1],
        {"ch": other},
    )
    swap.start()
    for axis, size, here, semaphores in (("tm", n_tm, tm, time_here), ("sub", n_sub, sub, sub_here)):
        for step, after, device in others(axis, size, here):

            @pl.when(jnp.logical_not(after))
            def _():
                pl.semaphore_signal(
                    semaphores.at[here], inc=1, device_id=device, device_id_type=MESH
                )

    list_along = [
        send(tiles_hbm.at[0, 0], own_list, list_send.at[step], list_recv.at[tm], device)
        for step, _, device in others("tm", n_tm, tm)
    ]
    for step, after, _ in others("tm", n_tm, tm):
        pl.when(jnp.logical_not(after))(list_along[step].start)
    for load in loads[:2]:
        load.wait()
    factor = precision_ref[...]
    series_ref[last] = jnp.zeros((2 * channels, LANES), jnp.bfloat16)
    series_ref[last, :, : M - 1] = whiten(factor, tail_ref[...])
    for load in loads[2:]:
        load.wait()
    swap.wait_recv()

    def chunk(owner, part):
        return series_ref.at[pl.ds((owner * 2 + part) * tiles, tiles)]

    mine = chunk(tm, ch)
    whitened = whiten(factor, raw_ref[...])
    for k in range(tiles):
        series_ref[(tm * 2 + ch) * tiles + k] = whitened[:, k * LANES : (k + 1) * LANES]
    along_time = [
        send(mine, mine, time_send.at[step], time_recv.at[tm], device)
        for step, _, device in others("tm", n_tm, tm)
    ]
    to_pair = []

    def forward(held):
        step = len(to_pair)
        copy = send(held, held, pair_send.at[step], pair_recv.at[step], {"ch": other})
        to_pair.append(copy)
        copy.start()

    for step, after, device in others("tm", n_tm, tm):

        @pl.when(after)
        def _():
            pl.semaphore_wait(time_here.at[device["tm"]], 1)
            list_along[step].start()

        along_time[step].start()
    forward(mine)
    lists_along = []
    for step in range(1, n_tm):
        if step == n_tm - 1:
            for back in range(1, n_tm):
                source = back + ((tm + n_tm - back) // n_tm) * (tm - 2 * back)
                held = lists_ref.at[sub, source]
                send(held, held, list_send.at[0], list_recv.at[source], {"ch": other}).wait_recv()
            held = lists_ref.at[sub]
            for at, after, device in others("sub", n_sub, sub):
                pl.when(after)(
                    functools.partial(pl.semaphore_wait, sub_here.at[device["sub"]], 1)
                )
                copy = send(held, held, lists_send.at[at], lists_recv.at[sub], device)
                lists_along.append(copy)
                copy.start()
        source = step + ((tm + n_tm - step) // n_tm) * (tm - 2 * step)
        held = chunk(source, ch)
        send(held, held, time_send.at[0], time_recv.at[source], {"ch": other}).wait_recv()
        forward(held)
    for at, _, device in others("sub", n_sub, sub):
        held = lists_ref.at[device["sub"]]
        send(held, held, lists_send.at[0], lists_recv.at[device["sub"]], {"ch": other}).wait_recv()
    for copy in to_pair:
        copy.wait_recv()
    for copy in [swap] + list_along + along_time + lists_along + to_pair:
        copy.wait_send()


def match_kernel(
    n_sub,
    series_ref,
    lists_ref,
    out_ref,
    lists_smem,
    work_smem,
    hankel_ref,
    lagged_ref,
    mine_ref,
    wide_ref,
    near_ref,
    products_ref,
    best_ref,
    list_sem,
):
    copy = pltpu.make_async_copy(lists_ref, lists_smem, list_sem)
    copy.start()
    units, unit_cols, depth = mine_ref.shape
    channels = depth // STEP
    n_tiles = unit_cols // LANES
    unit = unit_cols - M
    per_block = TS // LANES
    rows = TS + M
    ch = lax.axis_index("ch")
    me = lax.axis_index("tm") * n_sub + lax.axis_index("sub")
    own_tile = me * (units * unit // LANES)
    identity = (
        lax.broadcasted_iota(jnp.int32, (depth, depth), 0)
        == lax.broadcasted_iota(jnp.int32, (depth, depth), 1)
    )

    def lag(first_tile, count, scale):
        segment = jnp.concatenate([series_ref[first_tile + k] for k in range(count)], axis=1)
        segment = segment.astype(jnp.float32)
        width = count * LANES
        for l in range(STEP):
            moved = segment if l == 0 else pltpu.roll(segment, width - l, axis=1)
            hankel_ref[l * channels : (l + 1) * channels, :width] = moved.astype(jnp.bfloat16)
        scaled = jnp.where(identity, scale, 0.0).astype(jnp.bfloat16)
        lagged = []
        for at in range(0, width, depth):
            size = min(depth, width - at)
            lagged.append(
                lax.dot_general(
                    scaled[:size, :size] if size == depth else jnp.where(
                        lax.broadcasted_iota(jnp.int32, (size, size), 0)
                        == lax.broadcasted_iota(jnp.int32, (size, size), 1), scale, 0.0
                    ).astype(jnp.bfloat16),
                    hankel_ref[:, at : at + size],
                    (((1,), (1,)), ((), ())),
                    preferred_element_type=jnp.float32,
                ).astype(jnp.bfloat16)
            )
        norms = jnp.broadcast_to(jnp.sum(segment * segment, axis=0, keepdims=True), (8, width))
        shift = 1
        while shift < M:
            norms = norms + pltpu.roll(norms, width - shift, axis=1)
            shift *= 2
        return lagged, norms

    lagged, own_norms = lag(own_tile, units * unit // LANES + 1, 1.0)
    groups = [
        piece[at : at + STEP] for piece in lagged for at in range(0, piece.shape[0], STEP)
    ]
    for u in range(units):
        for q in range(unit_cols // STEP):
            place = ((q % n_tiles) * 8 + q // n_tiles) * STEP
            mine_ref[u, place : place + STEP, :] = groups[u * unit // STEP + q]
        best_ref[u] = jnp.full((8, unit_cols), jnp.inf, jnp.float32)
    lane = lax.broadcasted_iota(jnp.int32, (8, LANES), 1)
    own_at = [((lane // STEP) * n_tiles + t) * STEP + lane % STEP for t in range(n_tiles)]
    sublane = lax.broadcasted_iota(jnp.int32, (8, LANES), 0)

    copy.wait()
    owners, n_tm = lists_smem.shape[0] * lists_smem.shape[1], lists_smem.shape[1]

    def scan(owner, found):
        for slot in range(SLOTS):
            listed = (owner // n_tm, owner % n_tm, slot)
            row_block, col_block = lists_smem[(*listed, 0)], lists_smem[(*listed, 1)]
            for u in range(units):
                block = (own_tile * LANES + u * unit) // TS
                work_smem[found] = (row_block + col_block - block) * units + u
                hit = (row_block == block) | (col_block == block)
                found = found + hit.astype(jnp.int32)
        return found

    if owners <= 16:
        found = jnp.int32(0)
        for owner in range(owners):
            found = scan(owner, found)
    else:
        found = lax.fori_loop(0, owners, scan, jnp.int32(0))

    def ahead(tiles, at):
        turn = at // n_tiles
        tile = tiles[at % n_tiles]
        return tile if turn == 0 else pltpu.roll(tile, LANES - turn * STEP, axis=1)

    def keep_apart(offset):
        for g in range(0, (TS + M) // STEP, M // STEP):
            for at in range(g * STEP, (g + 1) * STEP, 8):
                for t in range(n_tiles):
                    here = (pl.ds(at, 8), pl.ds(t * LANES, LANES))
                    apart = (sublane + (at + offset)) - own_at[t]
                    products_ref[here] = jnp.where(
                        jnp.abs(apart) < EXCL, jnp.inf, products_ref[here]
                    )

    def reduce(u):
        run = TS // STEP

        def some(turn, low):
            part = turn % (STEP // 8)
            first = (turn // (STEP // 8)) * (run * STEP) + part * 8
            ones, twos, fours = {}, {}, {}
            low = list(low)
            for g in range(run + 7):
                ones[g] = [
                    products_ref[pl.ds(first + g * STEP, 8), t * LANES : (t + 1) * LANES]
                    for t in range(n_tiles)
                ]
                if g >= 1:
                    twos[g - 1] = [
                        ones[g - 1][t] + ahead(ones[g], t + 1) for t in range(n_tiles)
                    ]
                if g >= 3:
                    fours[g - 3] = [
                        twos[g - 3][t] + ahead(twos[g - 1], t + 2) for t in range(n_tiles)
                    ]
                if g >= 7:
                    wide = wide_ref[pl.ds(first + (g - 7) * STEP, 8), :]
                    for t in range(n_tiles):
                        score = fours[g - 7][t] + ahead(fours[g - 3], t + 4) + wide
                        low[t] = jnp.minimum(low[t], score)
            return tuple(low)

        low = tuple(best_ref[u, :, t * LANES : (t + 1) * LANES] for t in range(n_tiles))
        for turn in range(TS // run // STEP * (STEP // 8)):
            low = some(turn, low)
        for t in range(n_tiles):
            best_ref[u, :, t * LANES : (t + 1) * LANES] = low[t]

    def incidence(at, _):
        entry = work_smem[2 * at + ch]
        u = entry % units
        partner = entry // units
        lagged, norms = lag(partner * per_block, rows // LANES, -2.0)
        place = 0
        for piece in lagged:
            lagged_ref[place : place + piece.shape[0], :] = piece
            place += piece.shape[0]
        for k in range(per_block):
            one = jnp.broadcast_to(norms[:1, k * LANES : (k + 1) * LANES], (LANES, LANES))
            wide_ref[k * LANES : (k + 1) * LANES, :] = jnp.transpose(one)
        products_ref[...] = lax.dot_general(
            lagged_ref[...], mine_ref[u], (((1,), (1,)), ((), ())), preferred_element_type=jnp.float32
        )
        offset = partner * TS - (own_tile * LANES + u * unit)
        keep_apart(offset)
        reduce(u)
        return 0

    lax.fori_loop(0, (found + 1 - ch) // 2, incidence, 0)

    group = lane // STEP
    for u in range(units):
        low = jnp.min(best_ref[u], axis=0, keepdims=True)
        tiles = [
            jnp.broadcast_to(low[:, t * LANES : (t + 1) * LANES], (8, LANES)) for t in range(n_tiles)
        ]
        for k in range(unit // LANES):
            natural = None
            for g in range(LANES // STEP):
                q = k * (LANES // STEP) + g
                turn = (g - q // n_tiles) % (LANES // STEP)
                tile = tiles[q % n_tiles]
                tile = tile if turn == 0 else pltpu.roll(tile, turn * STEP, axis=1)
                natural = tile if natural is None else jnp.where(group == g, tile, natural)
            at = u * (unit // LANES) + k
            done = (natural[:1] + own_norms[:1, at * LANES : (at + 1) * LANES]) * (1.0 / DEPTH)
            out_ref[at : at + 1, :] = done


def swap_kernel(mine_ref, theirs_ref, sems):
    other = {"ch": 1 - lax.axis_index("ch")}
    barrier = pltpu.get_barrier_semaphore()
    pl.semaphore_signal(barrier, inc=1, device_id=other, device_id_type=MESH)
    pl.semaphore_wait(barrier, 1)
    copy = pltpu.make_async_remote_copy(
        src_ref=mine_ref,
        dst_ref=theirs_ref,
        send_sem=sems.at[0],
        recv_sem=sems.at[1],
        device_id=other,
        device_id_type=MESH,
    )
    copy.start()
    copy.wait()


def lower_kernel(mine_ref, theirs_ref, out_ref):
    out_ref[...] = jnp.minimum(mine_ref[...], theirs_ref[...])


def body(archive, tail, precision, tile_list):
    n_tm, n_sub = lax.axis_size("tm"), lax.axis_size("sub")
    owners = n_tm * n_sub
    channels, span = archive.shape
    piece = span // n_sub
    unit = min(piece, TS)
    units = piece // unit
    every = 2 * channels
    depth = STEP * every
    most = max(piece, TS) + M
    anywhere = pl.BlockSpec(memory_space=pltpu.HBM)
    inside = pl.BlockSpec(memory_space=pltpu.VMEM)
    series, lists = pl.pallas_call(
        functools.partial(gather_kernel, n_tm, n_sub),
        out_shape=[
            pltpu.VMEM((n_tm * span // LANES + 1, every, LANES), jnp.bfloat16),
            pltpu.VMEM((n_sub, n_tm) + tile_list.shape[2:], jnp.int32),
        ],
        in_specs=[anywhere] * 4,
        out_specs=[inside] * 2,
        scratch_shapes=[
            pltpu.VMEM(tail.shape, jnp.float32),
            pltpu.VMEM(precision.shape, jnp.float32),
            pltpu.VMEM((every, span // 2), jnp.float32),
            pltpu.SemaphoreType.DMA((4,)),
            pltpu.SemaphoreType.DMA((2,)),
            pltpu.SemaphoreType.DMA((n_tm,)),
            pltpu.SemaphoreType.DMA((n_tm,)),
            pltpu.SemaphoreType.DMA((n_tm,)),
            pltpu.SemaphoreType.DMA((n_tm,)),
            pltpu.SemaphoreType.DMA((n_tm,)),
            pltpu.SemaphoreType.DMA((n_tm,)),
            pltpu.SemaphoreType.DMA((n_sub,)),
            pltpu.SemaphoreType.DMA((n_sub,)),
            pltpu.SemaphoreType.REGULAR((n_tm,)),
            pltpu.SemaphoreType.REGULAR((n_sub,)),
        ],
        compiler_params=pltpu.CompilerParams(
            collective_id=0, has_side_effects=True, vmem_limit_bytes=62 * 2**20
        ),
    )(tile_list, archive, tail, precision)
    series = pltpu.with_memory_space_constraint(series, pltpu.VMEM)
    lists = pltpu.with_memory_space_constraint(lists, pltpu.VMEM)
    shape = (piece // LANES, LANES)
    mine = pl.pallas_call(
        functools.partial(match_kernel, n_sub),
        out_shape=pltpu.VMEM(shape, jnp.float32),
        in_specs=[inside] * 2,
        out_specs=inside,
        scratch_shapes=[
            pltpu.SMEM(lists.shape, jnp.int32),
            pltpu.SMEM((owners * SLOTS * units + 1,), jnp.int32),
            pltpu.VMEM((depth, most), jnp.bfloat16),
            pltpu.VMEM((TS + M, depth), jnp.bfloat16),
            pltpu.VMEM((units, unit + M, depth), jnp.bfloat16),
            pltpu.VMEM((TS, LANES), jnp.float32),
            pltpu.VMEM((8, LANES), jnp.float32),
            pltpu.VMEM((TS + M, unit + M), jnp.float32),
            pltpu.VMEM((units, 8, unit + M), jnp.float32),
            pltpu.SemaphoreType.DMA,
        ],
        compiler_params=pltpu.CompilerParams(vmem_limit_bytes=32 * 2**20),
    )(series, lists)
    mine = pltpu.with_memory_space_constraint(mine, pltpu.VMEM)
    theirs = pl.pallas_call(
        swap_kernel,
        out_shape=pltpu.VMEM(shape, jnp.float32),
        in_specs=[inside],
        out_specs=inside,
        scratch_shapes=[pltpu.SemaphoreType.DMA((2,))],
        compiler_params=pltpu.CompilerParams(
            collective_id=1, has_side_effects=True, vmem_limit_bytes=16 * 2**20
        ),
    )(mine)
    theirs = pltpu.with_memory_space_constraint(theirs, pltpu.VMEM)
    out = pl.pallas_call(
        lower_kernel,
        out_shape=jax.ShapeDtypeStruct(shape, jnp.float32),
        in_specs=[inside] * 2,
        out_specs=inside,
        compiler_params=pltpu.CompilerParams(vmem_limit_bytes=16 * 2**20),
    )(mine, theirs)
    return out.reshape(-1)


def solution(mesh):
    placed = (P("ch", ("grp", "tm")), P(None, "grp"), P(), P(("grp", "tm"), "sub", None, None))
    return jax.shard_map(
        body, mesh=mesh, in_specs=placed, out_specs=P(("grp", "tm", "sub")), check_vma=False
    )
```

time: 20.7 us -> 17.7 us (0.86)
  Pallas kernels: 19.2 us -> 17.6 us
  local copies, waits for them, and re-layouts: 1.28 us -> 0 us
    pallas_call x1 -> x4, Pallas kernels: 19.2 us -> 17.6 us  [the longest x1 11.4 us: body(): pl.pallas_call(functools.partial(gather_kernel, n_tm, n_sub), out_shape=[...]
    unnamed x1 -> x0, local copies, waits for them, and re-layouts: 1.28 us -> none
where the time goes in v1:
time: 17.7 us; the launch traced here: 17.6 us
  Pallas kernels  17.6 us (99%)
    pallas_call x1, Pallas kernels, body(): pl.pallas_call(functools.partial(gather_kernel, n_tm, n_sub), out_shape=[...  11.4 us
    pallas_call x1, Pallas kernels, body(): pl.pallas_call(functools.partial(match_kernel, n_sub), out_shape=pltpu.VM...  4.41 us
    pallas_call x1, Pallas kernels, body(): pl.pallas_call(swap_kernel, out_shape=pltpu.VMEM(shape, jnp.float32), in_...  1.22 us
    pallas_call x1, Pallas kernels, body(): pl.pallas_call(lower_kernel, out_shape=jax.ShapeDtypeStruct(shape, jnp.fl...  0.6 us

profile of v1, /device:TPU:0, one launch (start us, length us, event | category | flops | bytes accessed | tf_op | source)
XLA Modules:
  0.0 17.6 jit_solution(11864514422949197732)
XLA Ops:
  0.0 11.4 %shard_map.46 = (bf16[65,16,128]{2,1,0:T(8,128)(2,1)S(1)}, s32[2,4,2,2]{3,2,1,0:T(2,128)S(1)}) custom-call(s32[1,1,2,2]{3,2,1,0:T(2,128)} %tiles_hbm.1, f32[8,2048]{1,0:T(8,128)} %archive_hbm.1, f32[16,127]{1,0:T(8,128)} %tail_hbm.1, f32[16,16]{1,0:T(8,128)} %precision_hbm.1), custom_call_target="tpu_custom_call" | custom-call | tf_op jit(solution)/shard_map/pallas_call | solution.py:405
  11.4 4.4 %shard_map.47.mine_ref = f32[8,128]{1,0:T(8,128)S(1)} custom-call(bf16[65,16,128]{2,1,0:T(8,128)(2,1)S(1)} %get-tuple-element.7.series_ref, s32[2,4,2,2]{3,2,1,0:T(2,128)S(1)} %get-tuple-element.8.lists_ref), custom_call_target="tpu_custom_call" | custom-call | tf_op jit(solution)/shard_map/pallas_call | solution.py:437
  15.8 1.2 %shard_map.48.theirs_ref = f32[8,128]{1,0:T(8,128)S(1)} custom-call(f32[8,128]{1,0:T(8,128)S(1)} %shard_map.47.mine_ref), custom_call_target="tpu_custom_call" | custom-call | tf_op jit(solution)/shard_map/pallas_call | solution.py:457
  17.0 0.6 %shard_map.49 = f32[8,128]{1,0:T(8,128)} custom-call(f32[8,128]{1,0:T(8,128)S(1)} %shard_map.47.mine_ref, f32[8,128]{1,0:T(8,128)S(1)} %shard_map.48.theirs_ref), custom_call_target="tpu_custom_call" | custom-call | tf_op jit(solution)/shard_map/pallas_call | solution.py:468
